TPU v7x, 512 devices: a whole 4x4x16 slice. The times are simulated.
512 devices in a mesh: grp: 16 (over z_lo, x), fsdp: 4 (over y), tp: 8 (over z_hi, core).
Axes of the slice: x: 4, y: 4, z: 16 (z_hi: 4, z_lo: 4; z = z_hi * 4 + z_lo), core: 2. Of those that a mesh axis runs over, the one named last changes fastest.
Arguments:
- frames: bfloat16 [3072, 5120], P('fsdp', 'grp'), may hold values from -6 to 6
- projector: bfloat16 [5120, 8192], P('grp', 'tp'), may hold values from -0.078125 to 0.078125
- text_token_embedding: bfloat16 [16384, 8192], P(('grp', 'fsdp'), 'tp'), may hold values from -6 to 6
- norm_gain_vector: float32 [8192], replicated, may hold values from 0.1 to 1.9
- frozen: bfloat16 [8192, 1024], P('fsdp', 'tp'), may hold values from -0.0625 to 0.0625
- adapter_down_map: bfloat16 [8192, 64], P('fsdp'), may hold values from -0.0625 to 0.0625
- adapter_up_map: bfloat16 [64, 1024], P(None, 'tp'), may hold values from -0.75 to 0.75
- clip_frame_length: int32 [4, 16, 16], P('fsdp'), may hold values from 1 to 6, as said below
- audio_first_token: int32 [4, 16, 16], P('fsdp'), may hold values from 0 to 255, as said below
- segment_document_index: int32 [16384], P(('grp', 'fsdp')), may hold values from 0 to 255, never falling along the last dimension, each value on 1 to 256 neighbouring positions
- keep_document_flags: int32 [256], replicated, may hold values 0 or 1
- cotangent: bfloat16 [16384, 1024], P(('grp', 'fsdp'), 'tp'), may hold values from -0.046875 to 0.046875
Outputs:
- value_output: bfloat16 [16384, 1024], P(('grp', 'fsdp'), 'tp')
- projector_grad: float32 [5120, 8192], P('grp', 'tp')
- down_map_gradient: float32 [8192, 64], P('tp')
- up_map_gradient: float32 [64, 1024], P(None, 'tp')
Inputs may be any that keep to these rules, and one draw needn't show every extreme that they name: `clip_frame_length`: entry [f, g, k] is the length of clip k of frame block f * 16 + g; the 16 clips of a block sum to 48, and one of them has exactly 6 frames. `audio_first_token`: entry [f, g, k] is the first token, among the 256 tokens of block k * 4 + f, of the audio slots of clip k of frame block f * 16 + g; the 16 clips that one token block takes lie in distinct aligned windows of 16 tokens.
All inputs are finite; a program needn't handle non-finite values.
Results may differ from a plain program's by a relative error of at most 0.018.
Values may be sent and summed in bfloat16 or wider, within the bound.
No kernel may reach another device: no remote copies, remote signals or barrier semaphores. Data moves between devices by JAX's collectives and lax.ppermute only.
A program may use at most 128 MiB of HBM per device.

v0:
```python
import jax
import jax.numpy as jnp
from jax import lax
from jax.sharding import PartitionSpec as P

adapter_scale = 2.0
norm_eps = 1e-05


def in_blocks(x, dim, length):
    shape = x.shape
    blocks = x.reshape(*shape[:dim], length, shape[dim] // length, *shape[dim + 1 :])
    return jnp.moveaxis(blocks, dim, 0)


def sent_and_summed(x, axis, dim):
    length = lax.axis_size(axis)
    blocks = lax.all_to_all(in_blocks(x, dim, length), axis, 0, 0, tiled=True)
    return jnp.sum(blocks.astype(jnp.float32), axis=0)


def side_by_side(arrays, axis, dim, along):
    ends, at = ([], 0)
    for a in arrays[:-1]:
        at += a.shape[along]
        ends.append(at)
    both = jnp.concatenate(arrays, axis=along)
    return tuple(jnp.split(lax.all_gather(both, axis, axis=dim, tiled=True), ends, axis=along))


def copy_for_each(x, axis):
    copies = jnp.broadcast_to(x, (lax.axis_size(axis), *x.shape))
    return lax.all_to_all(copies, axis, split_axis=0, concat_axis=0, tiled=True)


def over_copies(x, axis):
    return copy_for_each(x, axis).astype(jnp.float32).sum(axis=0)


def rows_for(lines, length):
    spare = -len(lines) % length
    return jnp.pad(lines, [(0, spare)] + [(0, 0)] * (lines.ndim - 1))


def in_order(blocks, dim):
    shape = list(blocks.shape[1:])
    shape[dim] *= blocks.shape[0]
    return jnp.moveaxis(blocks, 0, dim).reshape(shape)


def collect(x, axis, dim):
    return in_order(copy_for_each(x, axis), dim)


def sum_at_owner(x, axis, dim):
    blocks = in_blocks(x, dim, lax.axis_size(axis))
    arrived = lax.all_to_all(blocks, axis, split_axis=0, concat_axis=0, tiled=True)
    return arrived.sum(axis=0)


def total_of(x, axes):
    padded = rows_for(x, lax.axis_size(axes))
    whole = collect(sum_at_owner(padded, axes, 0), axes, 0)
    return lax.slice_in_dim(whole, 0, len(x)).reshape(x.shape)


def together(arrays, axis):
    flat, at, outs = (jnp.concatenate([a.reshape(-1) for a in arrays]), 0, [])
    so_far = total_of(flat, axis)
    for a in arrays:
        outs.append(so_far[at : at + a.size].reshape(a.shape))
        at += a.size
    return tuple(outs)


def pick_entry(grid_in, position, which_axis):
    matches = lax.broadcasted_iota(jnp.int32, grid_in.shape, which_axis) == position
    return jnp.sum(jnp.where(matches, grid_in, 0), axis=which_axis)


def contract_leading(left_side, right_side):
    return lax.dot_general(
        left_side, right_side, (((0,), (0,)), ((), ())), preferred_element_type=jnp.float32
    )


def contract_trailing(left_side, right_side):
    return lax.dot_general(
        left_side, right_side, (((1,), (1,)), ((), ())), preferred_element_type=jnp.float32
    )


def shards(
    frames,
    projector,
    text_token_embedding,
    norm_gain_vector,
    frozen,
    adapter_down_map,
    adapter_up_map,
    clip_frame_length,
    audio_first_token,
    segment_document_index,
    keep_document_flags,
    cotangent,
):
    grp_index = lax.axis_index("grp")
    tensor_shard_index = lax.axis_index("tp")
    tok_count, tensor_shard_width = text_token_embedding.shape
    group_count = clip_frame_length.shape[1]
    frame_count = frames.shape[0] // group_count
    slot_cap = 2 * frame_count // group_count
    slot_total = group_count * slot_cap
    full_width = tensor_shard_width * lax.axis_size("tp")
    own_sizes = pick_entry(clip_frame_length[0], grp_index, 0)
    own_starts = jnp.cumsum(own_sizes) - own_sizes
    slot_offset = lax.broadcasted_iota(jnp.int32, (group_count, slot_cap), 1)
    frame_slot = own_starts[:, None] + slot_offset
    slot_live = slot_offset < own_sizes[:, None]
    frame_iota = lax.broadcasted_iota(jnp.int32, (group_count, slot_cap, frame_count), 2)
    sender = (
        ((frame_iota == frame_slot[:, :, None]) & slot_live[:, :, None])
        .astype(jnp.bfloat16)
        .reshape(slot_total, frame_count)
    )
    in_sizes = pick_entry(clip_frame_length[0], grp_index, 1)
    arrive_at = pick_entry(audio_first_token[0], grp_index, 1)
    token_iota = lax.broadcasted_iota(jnp.int32, (tok_count, group_count, slot_cap), 0)
    receive_mask = (token_iota == (arrive_at[:, None] + slot_offset)[None]) & (
        slot_offset < in_sizes[:, None]
    )[None]
    receiving_device = receive_mask.astype(jnp.bfloat16).reshape(tok_count, slot_total)
    is_audio = jnp.any(receive_mask, axis=(1, 2))
    embedded = sent_and_summed(
        jnp.dot(frames, projector, preferred_element_type=jnp.float32).astype(jnp.bfloat16),
        "grp",
        0,
    ).astype(jnp.bfloat16)
    outgoing = (
        jnp.dot(sender, embedded, preferred_element_type=jnp.float32)
        .astype(jnp.bfloat16)
        .reshape(group_count, slot_cap, tensor_shard_width)
    )
    incoming = lax.all_to_all(outgoing, "grp", split_axis=0, concat_axis=0, tiled=True).reshape(
        slot_total, tensor_shard_width
    )
    audio_part = jnp.dot(receiving_device, incoming, preferred_element_type=jnp.float32).astype(
        jnp.bfloat16
    )
    inputs = jnp.where(is_audio[:, None], audio_part, text_token_embedding)
    gathered = lax.all_gather(inputs, "tp", axis=1, tiled=True)
    widened = gathered.astype(jnp.float32)
    mean_sq = jnp.mean(widened * widened, axis=1)
    inv_rms = lax.rsqrt(mean_sq + norm_eps)
    normalized_input = (widened * inv_rms[:, None] * norm_gain_vector[None, :]).astype(jnp.bfloat16)
    frozen_complete, adapter_complete = side_by_side((frozen, adapter_down_map), "fsdp", 0, 1)
    base_output = jnp.dot(normalized_input, frozen_complete, preferred_element_type=jnp.float32)
    lower_rank_rows = jnp.dot(
        normalized_input, adapter_complete, preferred_element_type=jnp.float32
    )
    lower_halfway = lower_rank_rows.astype(jnp.bfloat16)
    value_output = (
        base_output
        + adapter_scale * jnp.dot(lower_halfway, adapter_up_map, preferred_element_type=jnp.float32)
    ).astype(jnp.bfloat16)
    doc_iota = lax.broadcasted_iota(jnp.int32, (tok_count, keep_document_flags.shape[0]), 1)
    weight_tok = jnp.sum(
        jnp.where(segment_document_index[:, None] == doc_iota, keep_document_flags[None, :], 0),
        axis=1,
    )
    output_gradient = cotangent * weight_tok.astype(jnp.bfloat16)[:, None]
    adapter_portion = adapter_scale * contract_trailing(output_gradient, adapter_up_map)
    dot_portion = jnp.sum(output_gradient.astype(jnp.float32) * base_output, axis=1) + jnp.sum(
        adapter_portion * lower_rank_rows, axis=1
    )
    adapter_gradient, row_dot_products = (
        over_copies(adapter_portion.astype(jnp.bfloat16), "tp").astype(jnp.float32),
        over_copies(dot_portion.astype(jnp.bfloat16), "tp").astype(jnp.float32),
    )
    adapter_halfway = adapter_gradient.astype(jnp.bfloat16)
    up_portion = adapter_scale * contract_leading(lower_halfway, output_gradient)
    local_normalized = lax.dynamic_slice_in_dim(
        normalized_input, tensor_shard_index * tensor_shard_width, tensor_shard_width, 1
    )
    down_portion = contract_leading(local_normalized, adapter_halfway)
    down_map_gradient, up_map_gradient = together((down_portion, up_portion), ("grp", "fsdp"))
    slot_grad = contract_leading(receiving_device, output_gradient).astype(jnp.bfloat16)
    slot_adapter = contract_leading(receiving_device, adapter_halfway).astype(jnp.bfloat16)
    slot_stats = lax.dot_general(
        receiving_device.astype(jnp.float32),
        jnp.stack([inv_rms, row_dot_products], axis=1),
        (((0,), (0,)), ((), ())),
        precision=lax.Precision.HIGHEST,
        preferred_element_type=jnp.float32,
    )
    spread_rows = contract_trailing(slot_grad, frozen_complete)
    reduced_result = lax.psum_scatter(
        spread_rows.astype(jnp.bfloat16), "tp", scatter_dimension=1, tiled=True
    ).astype(jnp.float32)
    local_adapter = lax.dynamic_slice_in_dim(
        adapter_complete, tensor_shard_index * tensor_shard_width, tensor_shard_width, 0
    )
    gradient_norm = reduced_result + contract_trailing(slot_adapter, local_adapter)
    own_gain = lax.dynamic_slice_in_dim(
        norm_gain_vector, tensor_shard_index * tensor_shard_width, tensor_shard_width, 0
    )
    slot_inv = slot_stats[:, 0:1]
    slot_dot = slot_stats[:, 1:2]
    grad_rows = (
        slot_inv * own_gain[None, :] * gradient_norm
        - incoming.astype(jnp.float32) * (slot_inv * slot_inv * slot_dot / full_width)
    ).astype(jnp.bfloat16)
    returned = lax.all_to_all(
        grad_rows.reshape(group_count, slot_cap, tensor_shard_width),
        "grp",
        split_axis=0,
        concat_axis=0,
        tiled=True,
    ).reshape(slot_total, tensor_shard_width)
    frame_grad = contract_leading(sender, returned).astype(jnp.bfloat16)
    proj_part = contract_leading(frames, collect(frame_grad, "grp", 0))
    projector_grad = over_copies(proj_part.astype(jnp.bfloat16), "fsdp").astype(jnp.float32)
    return (value_output, projector_grad, down_map_gradient, up_map_gradient)


def solution(mesh):
    in_specs = (
        P("fsdp", "grp"),
        P("grp", "tp"),
        P(("grp", "fsdp"), "tp"),
        P(),
        P("fsdp", "tp"),
        P("fsdp", None),
        P(None, "tp"),
        P("fsdp", None, None),
        P("fsdp", None, None),
        P(("grp", "fsdp")),
        P(),
        P(("grp", "fsdp"), "tp"),
    )
    out_specs = (P(("grp", "fsdp"), "tp"), P("grp", "tp"), P("tp", None), P(None, "tp"))
    return jax.shard_map(shards, mesh=mesh, in_specs=in_specs, out_specs=out_specs, check_vma=False)
```

profile of v0, /device:TPU:64, one launch (start us, length us, event | category | flops | bytes accessed | tf_op | source)
XLA Modules:
  0.0 395.2 jit_solution(4861010309446714678)
XLA Ops:
  8.3 3.2 convolution_convert_fusion.1
  11.5 8.7 %all-to-all-start = ((bf16[16,48,1024]{2,1,0:T(8,128)(2,1)}), bf16[16,48,1024]{2,1,0:T(8,128)(2,1)S(1)}, u32[]{:S(2)}, u32[]{:S(2)}) async-start(bf16[16,48,1024]{2,1,0:T(8,128)(2,1)} %bitcast.51), calls=%async_computation | async-start | bytes 3145728 | tf_op jit(solution)/shard_map/all_to_all | solution.py:18
  23.2 33.4 %all-to-all-done = bf16[16,48,1024]{2,1,0:T(8,128)(2,1)S(1)} async-done(((bf16[16,48,1024]{2,1,0:T(8,128)(2,1)}), bf16[16,48,1024]{2,1,0:T(8,128)(2,1)S(1)}, u32[]{:S(2)}, u32[]{:S(2)}) %all-to-all-start) | async-done | bytes 1572896 | tf_op jit(solution)/shard_map/all_to_all | solution.py:18
  58.0 5.1 %all-to-all-start.1 = ((bf16[16,6,1024]{2,1,0:T(8,128)(2,1)}), bf16[16,6,1024]{2,1,0:T(8,128)(2,1)S(1)}, u32[]{:S(2)}, u32[]{:S(2)}) async-start(bf16[16,6,1024]{2,1,0:T(8,128)(2,1)} %reshape.193), calls=%async_computation.1 | async-start | bytes 524288 | tf_op jit(solution)/shard_map/all_to_all | solution.py:144
  63.3 7.9 %all-to-all-done.1 = bf16[16,6,1024]{2,1,0:T(8,128)(2,1)S(1)} async-done(((bf16[16,6,1024]{2,1,0:T(8,128)(2,1)}), bf16[16,6,1024]{2,1,0:T(8,128)(2,1)S(1)}, u32[]{:S(2)}, u32[]{:S(2)}) %all-to-all-start.1) | async-done | bytes 196640 | tf_op jit(solution)/shard_map/all_to_all | solution.py:144
  73.8 7.2 %all-gather.5.cloned.1.call-done = bf16[8192,192]{1,0:T(8,128)(2,1)} async-done(((bf16[2048,192]{1,0:T(8,128)(2,1)}), bf16[8192,192]{1,0:T(8,128)(2,1)}) %all-gather.5.cloned.1.call-update) | async-done | bytes 3145744 | tf_op jit(solution)/shard_map/all_gather | solution.py:28
  81.1 3.8 convolution_convert_fusion
  84.9 92.6 %all-gather.3.cloned.1.call-done = bf16[256,8192]{1,0:T(8,128)(2,1)} async-done(((bf16[256,1024]{1,0:T(8,128)(2,1)}), bf16[256,8192]{1,0:T(8,128)(2,1)}) %all-gather.3.cloned.1.call-update) | async-done | bytes 4194320 | tf_op jit(solution)/shard_map/all_gather | solution.py:151
  177.5 3.3 fusion
  187.9 16.1 %all_to_all.51 = bf16[8,2,128]{2,1,0:T(2,128)(2,1)S(1)} all-to-all(bf16[8,2,128]{2,1,0:T(2,128)(2,1)S(1)} %reshape.203), channel_id=1, replica_groups=mesh['grp'=16,'fsdp'=4,'tp'=8] {'tp'}, dimensions={0} | all-to-all | bytes 8192 | tf_op jit(solution)/shard_map/all_to_all | solution.py:33
  204.6 4.0 %all-to-all-start.3 = ((bf16[8,256,64]{1,2,0:T(8,128)(2,1)}), bf16[8,256,64]{1,2,0:T(8,128)(2,1)}, u32[]{:S(2)}, u32[]{:S(2)}) async-start(bf16[8,256,64]{1,2,0:T(8,128)(2,1)} %broadcast_in_dim.61), calls=%async_computation.4 | async-start | bytes 524288 | tf_op jit(solution)/shard_map/all_to_all | solution.py:33
  211.0 18.4 %all-to-all-done.3 = bf16[8,256,64]{1,2,0:T(8,128)(2,1)} async-done(((bf16[8,256,64]{1,2,0:T(8,128)(2,1)}), bf16[8,256,64]{1,2,0:T(8,128)(2,1)}, u32[]{:S(2)}, u32[]{:S(2)}) %all-to-all-start.3) | async-done | bytes 262176 | tf_op jit(solution)/shard_map/all_to_all | solution.py:33
  232.6 15.0 %reduce-scatter.2.cloned.1.call-done = bf16[96,1024]{1,0:T(8,128)(2,1)} async-done(((bf16[96,8192]{1,0:T(8,128)(2,1)}), bf16[96,1024]{1,0:T(8,128)(2,1)}) %reduce-scatter.2.cloned.1.call-update) | async-done | bytes 196624 | tf_op jit(solution)/shard_map/reduce_scatter | solution.py:197
  250.0 7.0 %all-to-all-start.4 = ((bf16[16,6,1024]{2,1,0:T(8,128)(2,1)}), bf16[16,6,1024]{2,1,0:T(8,128)(2,1)S(1)}, u32[]{:S(2)}, u32[]{:S(2)}) async-start(bf16[16,6,1024]{2,1,0:T(8,128)(2,1)} %reshape.194), calls=%async_computation.5 | async-start | bytes 524288 | tf_op jit(solution)/shard_map/all_to_all | solution.py:213
  258.7 6.0 %all-to-all-done.4 = bf16[16,6,1024]{2,1,0:T(8,128)(2,1)S(1)} async-done(((bf16[16,6,1024]{2,1,0:T(8,128)(2,1)}), bf16[16,6,1024]{2,1,0:T(8,128)(2,1)S(1)}, u32[]{:S(2)}, u32[]{:S(2)}) %all-to-all-start.4) | async-done | bytes 196640 | tf_op jit(solution)/shard_map/all_to_all | solution.py:213
  264.6 12.8 %all-to-all-start.7 = ((f32[64,1,1152]{2,1,0:T(1,128)}), f32[64,1,1152]{2,1,0:T(1,128)S(1)}, u32[]{:S(2)}, u32[]{:S(2)}) async-start(f32[64,1,1152]{2,1,0:T(1,128)} %bitcast.13), calls=%async_computation.8 | async-start | bytes 589824 | tf_op jit(solution)/shard_map/all_to_all | solution.py:57
  278.0 11.3 %all-to-all-done.7 = f32[64,1,1152]{2,1,0:T(1,128)S(1)} async-done(((f32[64,1,1152]{2,1,0:T(1,128)}), f32[64,1,1152]{2,1,0:T(1,128)S(1)}, u32[]{:S(2)}, u32[]{:S(2)}) %all-to-all-start.7) | async-done | bytes 294944 | tf_op jit(solution)/shard_map/all_to_all | solution.py:57
  290.7 5.7 %all-to-all-start.5 = ((bf16[16,48,1024]{2,1,0:T(8,128)(2,1)}), bf16[16,48,1024]{2,1,0:T(8,128)(2,1)S(1)}, u32[]{:S(2)}, u32[]{:S(2)}) async-start(bf16[16,48,1024]{2,1,0:T(8,128)(2,1)} %broadcast_in_dim.62), calls=%async_computation.6 | async-start | bytes 3145728 | tf_op jit(solution)/shard_map/all_to_all | solution.py:33
  296.6 35.8 %all-to-all-done.5 = bf16[16,48,1024]{2,1,0:T(8,128)(2,1)S(1)} async-done(((bf16[16,48,1024]{2,1,0:T(8,128)(2,1)}), bf16[16,48,1024]{2,1,0:T(8,128)(2,1)S(1)}, u32[]{:S(2)}, u32[]{:S(2)}) %all-to-all-start.5) | async-done | bytes 1572896 | tf_op jit(solution)/shard_map/all_to_all | solution.py:33
  333.2 6.7 %all-to-all-start.8 = ((f32[64,1,1152]{2,1,0:T(1,128)}), f32[64,1,1152]{2,1,0:T(1,128)S(1)}, u32[]{:S(2)}, u32[]{:S(2)}) async-start(f32[64,1,1152]{2,1,0:T(1,128)} %broadcast_in_dim.64), calls=%async_computation.9 | async-start | bytes 589824 | tf_op jit(solution)/shard_map/all_to_all | solution.py:33
  341.6 8.8 %all-to-all-done.8 = f32[64,1,1152]{2,1,0:T(1,128)S(1)} async-done(((f32[64,1,1152]{2,1,0:T(1,128)}), f32[64,1,1152]{2,1,0:T(1,128)S(1)}, u32[]{:S(2)}, u32[]{:S(2)}) %all-to-all-start.8) | async-done | bytes 294944 | tf_op jit(solution)/shard_map/all_to_all | solution.py:33
  352.3 3.7 all-to-all-start.6
  356.9 2.4 reduce.5
  366.4 20.7 %all-to-all-done.6 = bf16[4,320,1024]{2,1,0:T(8,128)(2,1)S(1)} async-done(((bf16[4,320,1024]{2,1,0:T(8,128)(2,1)}), bf16[4,320,1024]{2,1,0:T(8,128)(2,1)S(1)}, u32[]{:S(2)}, u32[]{:S(2)}) %all-to-all-start.6) | async-done | bytes 2621472 | tf_op jit(solution)/shard_map/all_to_all | solution.py:33
  (119 shorter events, 41.6 us)
Async XLA Ops:
  7.2 13.0 %copy-start.6 = (bf16[2048,64]{0,1:T(8,128)(2,1)S(1)}, bf16[2048,64]{0,1:T(8,128)(2,1)}, u32[]{:S(2)}) copy-start(bf16[2048,64]{0,1:T(8,128)(2,1)} %param.17) | copy-start | bytes 786436
  7.2 13.3 %copy-start.5 = (bf16[2048,128]{1,0:T(8,128)(2,1)S(1)}, bf16[2048,128]{1,0:T(8,128)(2,1)}, u32[]{:S(2)}) copy-start(bf16[2048,128]{1,0:T(8,128)(2,1)} %param.16) | copy-start | bytes 1572868
  11.5 10.3 %copy-start.12 = (s32[1,16,16]{2,1,0:T(8,128)S(1)}, s32[1,16,16]{2,1,0:T(8,128)}, u32[]{:S(2)}) copy-start(s32[1,16,16]{2,1,0:T(8,128)} %param.19) | copy-start | bytes 3076
  11.5 10.3 %copy-start.13 = (s32[1,16,16]{2,1,0:T(8,128)S(1)}, s32[1,16,16]{2,1,0:T(8,128)}, u32[]{:S(2)}) copy-start(s32[1,16,16]{2,1,0:T(8,128)} %param.20) | copy-start | bytes 3076
  11.5 45.2 %all-to-all-start = ((bf16[16,48,1024]{2,1,0:T(8,128)(2,1)}), bf16[16,48,1024]{2,1,0:T(8,128)(2,1)S(1)}, u32[]{:S(2)}, u32[]{:S(2)}) async-start(bf16[16,48,1024]{2,1,0:T(8,128)(2,1)} %bitcast.51), calls=%async_computation | async-start | bytes 3145728 | tf_op jit(solution)/shard_map/all_to_all | solution.py:18
  20.2 60.9 %all-gather.5.cloned.1.call-start = ((), (), s32[]{:S(2)}) async-start(), calls=%async_computation.11 | async-start | bytes 5242880 | tf_op jit(solution)/shard_map/all_gather | solution.py:28
  21.7 51.8 %copy-start.7 = (bf16[256,128]{1,0:T(8,128)(2,1)S(1)}, bf16[256,128]{1,0:T(8,128)(2,1)}, u32[]{:S(2)}) copy-start(bf16[256,128]{1,0:T(8,128)(2,1)} %param.23) | copy-start | bytes 196612
  21.7 51.9 %copy-start.18 = (s32[256]{0:T(256)S(1)}, s32[256]{0:T(256)}, u32[]{:S(2)}) copy-start(s32[256]{0:T(256)} %param.22) | copy-start | bytes 3076
  21.7 51.9 %copy-start.19 = (s32[256]{0:T(256)S(1)}, s32[256]{0:T(256)}, u32[]{:S(2)}) copy-start(s32[256]{0:T(256)} %param.21) | copy-start | bytes 3076
  23.2 187.1 %copy-start.14 = (s32[96]{0:T(128)}, s32[96]{0:T(128)S(1)}, u32[]{:S(2)}) copy-start(s32[96]{0:T(128)S(1)} %get-tuple-element.41) | copy-start | bytes 1156
  23.2 187.1 %copy-start.15 = (pred[96]{0:T(512)(128)(4,1)}, pred[96]{0:T(512)(128)(4,1)S(1)}, u32[]{:S(2)}) copy-start(pred[96]{0:T(512)(128)(4,1)S(1)} %get-tuple-element.39) | copy-start | bytes 292
  58.0 13.2 %all-to-all-start.1 = ((bf16[16,6,1024]{2,1,0:T(8,128)(2,1)}), bf16[16,6,1024]{2,1,0:T(8,128)(2,1)S(1)}, u32[]{:S(2)}, u32[]{:S(2)}) async-start(bf16[16,6,1024]{2,1,0:T(8,128)(2,1)} %reshape.193), calls=%async_computation.1 | async-start | bytes 524288 | tf_op jit(solution)/shard_map/all_to_all | solution.py:144
  63.1 114.4 %all-gather.3.cloned.1.call-start = ((), (), s32[]{:S(2)}) async-start(), calls=%async_computation.10 | async-start | bytes 4718592 | tf_op jit(solution)/shard_map/all_gather | solution.py:151
  73.4 174.2 %reduce-scatter.2.cloned.1.call-start = ((), (), s32[]{:S(2)}) async-start(), calls=%async_computation.12 | async-start | bytes 1769472 | tf_op jit(solution)/shard_map/reduce_scatter | solution.py:197
  84.9 95.9 %copy-start.9 = (f32[8192]{0:T(1024)S(1)}, f32[8192]{0:T(1024)}, u32[]{:S(2)}) copy-start(f32[8192]{0:T(1024)} %param.15) | copy-start | bytes 98308
  204.6 24.8 %all-to-all-start.3 = ((bf16[8,256,64]{1,2,0:T(8,128)(2,1)}), bf16[8,256,64]{1,2,0:T(8,128)(2,1)}, u32[]{:S(2)}, u32[]{:S(2)}) async-start(bf16[8,256,64]{1,2,0:T(8,128)(2,1)} %broadcast_in_dim.61), calls=%async_computation.4 | async-start | bytes 524288 | tf_op jit(solution)/shard_map/all_to_all | solution.py:33
  209.3 38.4 %slice-start = ((bf16[8192,192]{1,0:T(8,128)(2,1)}), bf16[8192,64]{1,0:T(8,128)(2,1)S(1)}, s32[]{:S(2)}) async-start(bf16[8192,192]{1,0:T(8,128)(2,1)} %all-gather.5.cloned.1.call-done), calls=%async_computation.13 | async-start | bytes 4194304 | tf_op jit(solution)/shard_map/split | solution.py:28
  232.6 44.8 %copy-start.17 = (s32[16]{0:T(128)S(1)}, s32[16]{0:T(128)}, u32[]{:S(2)}) copy-start(s32[16]{0:T(128)} %copy-done.16) | copy-start | bytes 196
  232.6 44.9 %copy-start.11 = (s32[16]{0:T(128)S(1)}, s32[16]{0:T(128)}, u32[]{:S(2)}) copy-start(s32[16]{0:T(128)} %copy-done.10) | copy-start | bytes 196
  250.0 14.7 %all-to-all-start.4 = ((bf16[16,6,1024]{2,1,0:T(8,128)(2,1)}), bf16[16,6,1024]{2,1,0:T(8,128)(2,1)S(1)}, u32[]{:S(2)}, u32[]{:S(2)}) async-start(bf16[16,6,1024]{2,1,0:T(8,128)(2,1)} %reshape.194), calls=%async_computation.5 | async-start | bytes 524288 | tf_op jit(solution)/shard_map/all_to_all | solution.py:213
  264.6 24.7 %all-to-all-start.7 = ((f32[64,1,1152]{2,1,0:T(1,128)}), f32[64,1,1152]{2,1,0:T(1,128)S(1)}, u32[]{:S(2)}, u32[]{:S(2)}) async-start(f32[64,1,1152]{2,1,0:T(1,128)} %bitcast.13), calls=%async_computation.8 | async-start | bytes 589824 | tf_op jit(solution)/shard_map/all_to_all | solution.py:57
  290.7 41.7 %all-to-all-start.5 = ((bf16[16,48,1024]{2,1,0:T(8,128)(2,1)}), bf16[16,48,1024]{2,1,0:T(8,128)(2,1)S(1)}, u32[]{:S(2)}, u32[]{:S(2)}) async-start(bf16[16,48,1024]{2,1,0:T(8,128)(2,1)} %broadcast_in_dim.62), calls=%async_computation.6 | async-start | bytes 3145728 | tf_op jit(solution)/shard_map/all_to_all | solution.py:33
  333.2 17.2 %all-to-all-start.8 = ((f32[64,1,1152]{2,1,0:T(1,128)}), f32[64,1,1152]{2,1,0:T(1,128)S(1)}, u32[]{:S(2)}, u32[]{:S(2)}) async-start(f32[64,1,1152]{2,1,0:T(1,128)} %broadcast_in_dim.64), calls=%async_computation.9 | async-start | bytes 589824 | tf_op jit(solution)/shard_map/all_to_all | solution.py:33
  352.3 34.9 %all-to-all-start.6 = ((bf16[4,320,1024]{2,1,0:T(8,128)(2,1)}), bf16[4,320,1024]{2,1,0:T(8,128)(2,1)S(1)}, u32[]{:S(2)}, u32[]{:S(2)}) async-start(bf16[4,320,1024]{2,1,0:T(8,128)(2,1)} %broadcast_in_dim.63), calls=%async_computation.7 | async-start | bytes 5242880 | tf_op jit(solution)/shard_map/all_to_all | solution.py:33
  (8 other events, 13.8 us)
Sparse Core Ops, SparseCore 0:
  23.7 57.3 all-gather.4
  83.2 94.2 all-gather.2
  180.3 67.2 reduce-scatter.1
where the time goes:
time: 397 us; the launch traced here: 395 us
  waiting for transfers between devices  257 us (65%)
  starting transfers between devices  53.8 us (14%)
  local copies, waits for them, and re-layouts  21.2 us (5%)
  matrix products  18 us (5%)
  blocking collectives  16.1 us (4%)
  other arithmetic  14.8 us (4%)
  between operations  14.1 us (4%)
    all_gather x1, waiting for transfers between devices, shards(): gathered = lax.all_gather(inputs, 'tp', axis=1, tiled=True)  92.6 us
    all_to_all x4, waiting for transfers between devices, copy_for_each(): return lax.all_to_all(copies, axis, split_axis=0, concat_axis=0, tiled=True)  83.7 us
    all_to_all x1, waiting for transfers between devices, sent_and_summed(): blocks = lax.all_to_all(in_blocks(x, dim, length), axis, 0, 0, tiled=True)  33.4 us
    all_to_all x4, starting transfers between devices, copy_for_each(): return lax.all_to_all(copies, axis, split_axis=0, concat_axis=0, tiled=True)  20 us
    all_to_all x1, blocking collectives, copy_for_each(): return lax.all_to_all(copies, axis, split_axis=0, concat_axis=0, tiled=True)  16.1 us
    reduce_scatter x1, waiting for transfers between devices, shards(): lax.psum_scatter(spread_rows.astype(jnp.bfloat16), 'tp', scatter_dimensio...  15 us
    all_to_all x1, starting transfers between devices, sum_at_owner(): lax.all_to_all(blocks, axis, split_axis=0, concat_axis=0, tiled=True)  12.8 us
    all_to_all x1, waiting for transfers between devices, sum_at_owner(): lax.all_to_all(blocks, axis, split_axis=0, concat_axis=0, tiled=True)  11.3 us
  transfers between devices with their start and end apart: 11, of which 11 were waited for; matrix products, arithmetic and copies ran while one was open for 10% of the time, Pallas kernels for 0%

commit v1 on v0

--- a/solution.py
+++ b/solution.py
@@ -148,7 +148,10 @@
         jnp.bfloat16
     )
     inputs = jnp.where(is_audio[:, None], audio_part, text_token_embedding)
-    gathered = lax.all_gather(inputs, "tp", axis=1, tiled=True)
+    size = lax.axis_size("tp")
+    pieces = jnp.stack([inputs for _ in range(size)])
+    pieces = lax.all_to_all(pieces, "tp", split_axis=0, concat_axis=0)
+    gathered = jnp.concatenate(pieces, axis=1)
     widened = gathered.astype(jnp.float32)
     mean_sq = jnp.mean(widened * widened, axis=1)
     inv_rms = lax.rsqrt(mean_sq + norm_eps)

time: 397 us -> 496 us (1.25)
  waiting for transfers between devices: 257 us -> 350 us
  starting transfers between devices: 53.8 us -> 59.3 us
    all_to_all x0 -> x1, waiting for transfers between devices: none -> 148 us  [shards(): pieces = lax.all_to_all(pieces, 'tp', split_axis=0, concat_axis=0)]
    all_gather x1 -> x0, waiting for transfers between devices: 92.6 us -> none  [shards(): gathered = lax.all_gather(inputs, 'tp', axis=1, tiled=True)]
    all_gather x1, waiting for transfers between devices: 7.23 us -> 58.6 us  [side_by_side(): lax.all_gather(both, axis, axis=dim, tiled=True)]
    reduce_scatter x1, waiting for transfers between devices: 15 us -> 0.02 us  [shards(): lax.psum_scatter(spread_rows.astype(jnp.bfloat16), 'tp', scatter_dimensio...]
    all_to_all x0 -> x1, starting transfers between devices: none -> 12.5 us  [shards(): pieces = lax.all_to_all(pieces, 'tp', split_axis=0, concat_axis=0)]
  transfers between devices with their start and end apart: 11 -> 11, of which waited for: 11 -> 10; matrix products, arithmetic and copies ran while one was open for 10% -> 7% of each run, Pallas kernels for 0% -> 0%
where the time goes in v1:
time: 496 us; the launch traced here: 495 us
  waiting for transfers between devices  350 us (71%)
  starting transfers between devices  59.3 us (12%)
  local copies, waits for them, and re-layouts  23.2 us (5%)
  matrix products  17.4 us (4%)
  other arithmetic  15.5 us (3%)
  blocking collectives  14.8 us (3%)
  between operations  14.5 us (3%)
    all_to_all x1, waiting for transfers between devices, shards(): pieces = lax.all_to_all(pieces, 'tp', split_axis=0, concat_axis=0)  148 us
    all_to_all x4, waiting for transfers between devices, copy_for_each(): return lax.all_to_all(copies, axis, split_axis=0, concat_axis=0, tiled=True)  83.2 us
    all_gather x1, waiting for transfers between devices, side_by_side(): lax.all_gather(both, axis, axis=dim, tiled=True)  58.6 us
    all_to_all x1, waiting for transfers between devices, sent_and_summed(): blocks = lax.all_to_all(in_blocks(x, dim, length), axis, 0, 0, tiled=True)  35 us
    all_to_all x4, starting transfers between devices, copy_for_each(): return lax.all_to_all(copies, axis, split_axis=0, concat_axis=0, tiled=True)  19.9 us
    all_to_all x1, blocking collectives, copy_for_each(): return lax.all_to_all(copies, axis, split_axis=0, concat_axis=0, tiled=True)  14.8 us
    all_to_all x1, starting transfers between devices, shards(): pieces = lax.all_to_all(pieces, 'tp', split_axis=0, concat_axis=0)  12.5 us
    all_to_all x1, waiting for transfers between devices, sum_at_owner(): lax.all_to_all(blocks, axis, split_axis=0, concat_axis=0, tiled=True)  10.1 us
  transfers between devices with their start and end apart: 11, of which 10 were waited for; matrix products, arithmetic and copies ran while one was open for 7% of the time, Pallas kernels for 0%

profile of v1, /device:TPU:64, one launch (start us, length us, event | category | flops | bytes accessed | tf_op | source)
XLA Modules:
  0.0 494.6 jit_solution(1897537474639367126)
XLA Ops:
  8.3 3.2 convolution_convert_fusion.1
  11.5 8.6 %all-to-all-start = ((bf16[16,48,1024]{2,1,0:T(8,128)(2,1)}), bf16[16,48,1024]{2,1,0:T(8,128)(2,1)S(1)}, u32[]{:S(2)}, u32[]{:S(2)}) async-start(bf16[16,48,1024]{2,1,0:T(8,128)(2,1)} %bitcast.59), calls=%async_computation | async-start | bytes 3145728 | tf_op jit(solution)/shard_map/all_to_all | solution.py:18
  21.5 35.0 %all-to-all-done = bf16[16,48,1024]{2,1,0:T(8,128)(2,1)S(1)} async-done(((bf16[16,48,1024]{2,1,0:T(8,128)(2,1)}), bf16[16,48,1024]{2,1,0:T(8,128)(2,1)S(1)}, u32[]{:S(2)}, u32[]{:S(2)}) %all-to-all-start) | async-done | bytes 1572896 | tf_op jit(solution)/shard_map/all_to_all | solution.py:18
  57.8 5.1 %all-to-all-start.1 = ((bf16[16,6,1024]{2,1,0:T(8,128)(2,1)}), bf16[16,6,1024]{2,1,0:T(8,128)(2,1)S(1)}, u32[]{:S(2)}, u32[]{:S(2)}) async-start(bf16[16,6,1024]{2,1,0:T(8,128)(2,1)} %reshape.199), calls=%async_computation.1 | async-start | bytes 524288 | tf_op jit(solution)/shard_map/all_to_all | solution.py:144
  63.1 7.8 %all-to-all-done.1 = bf16[16,6,1024]{2,1,0:T(8,128)(2,1)S(1)} async-done(((bf16[16,6,1024]{2,1,0:T(8,128)(2,1)}), bf16[16,6,1024]{2,1,0:T(8,128)(2,1)S(1)}, u32[]{:S(2)}, u32[]{:S(2)}) %all-to-all-start.1) | async-done | bytes 196640 | tf_op jit(solution)/shard_map/all_to_all | solution.py:144
  74.8 12.5 %all-to-all-start.2 = ((bf16[8,256,1024]{1,2,0:T(8,128)(2,1)}), bf16[8,256,1024]{1,2,0:T(8,128)(2,1)}, u32[]{:S(2)}, u32[]{:S(2)}) async-start(bf16[8,256,1024]{1,2,0:T(8,128)(2,1)} %stack.6), calls=%async_computation.2 | async-start | bytes 8388608 | tf_op jit(solution)/shard_map/all_to_all | solution.py:153
  89.2 58.6 %all-gather.2.cloned.1.call-done = bf16[8192,192]{1,0:T(8,128)(2,1)} async-done(((bf16[2048,192]{1,0:T(8,128)(2,1)}), bf16[8192,192]{1,0:T(8,128)(2,1)}) %all-gather.2.cloned.1.call-update) | async-done | bytes 3145744 | tf_op jit(solution)/shard_map/all_gather | solution.py:28
  147.8 3.8 convolution_convert_fusion
  151.6 148.3 %all-to-all-done.2 = bf16[8,256,1024]{1,2,0:T(8,128)(2,1)} async-done(((bf16[8,256,1024]{1,2,0:T(8,128)(2,1)}), bf16[8,256,1024]{1,2,0:T(8,128)(2,1)}, u32[]{:S(2)}, u32[]{:S(2)}) %all-to-all-start.2) | async-done | bytes 4194336 | tf_op jit(solution)/shard_map/all_to_all | solution.py:153
  299.9 3.3 multiply_reduce_fusion
  303.3 3.0 fusion.1
  311.5 14.8 %all_to_all.56 = bf16[8,2,128]{2,1,0:T(2,128)(2,1)S(1)} all-to-all(bf16[8,2,128]{2,1,0:T(2,128)(2,1)S(1)} %reshape.210), channel_id=1, replica_groups=mesh['grp'=16,'fsdp'=4,'tp'=8] {'tp'}, dimensions={0} | all-to-all | bytes 8192 | tf_op jit(solution)/shard_map/all_to_all | solution.py:33
  327.1 3.4 all-to-all-start.4
  333.5 18.3 %all-to-all-done.4 = bf16[8,256,64]{1,2,0:T(8,128)(2,1)S(1)} async-done(((bf16[8,256,64]{1,2,0:T(8,128)(2,1)}), bf16[8,256,64]{1,2,0:T(8,128)(2,1)S(1)}, u32[]{:S(2)}, u32[]{:S(2)}) %all-to-all-start.4) | async-done | bytes 262176 | tf_op jit(solution)/shard_map/all_to_all | solution.py:33
  356.2 4.2 all-to-all-start.5
  361.9 6.8 %all-to-all-done.5 = bf16[16,6,1024]{2,1,0:T(8,128)(2,1)S(1)} async-done(((bf16[16,6,1024]{2,1,0:T(8,128)(2,1)}), bf16[16,6,1024]{2,1,0:T(8,128)(2,1)S(1)}, u32[]{:S(2)}, u32[]{:S(2)}) %all-to-all-start.5) | async-done | bytes 196640 | tf_op jit(solution)/shard_map/all_to_all | solution.py:216
  368.7 8.9 %all-to-all-start.8 = ((f32[64,1,1152]{2,1,0:T(1,128)}), f32[64,1,1152]{2,1,0:T(1,128)S(1)}, u32[]{:S(2)}, u32[]{:S(2)}) async-start(f32[64,1,1152]{2,1,0:T(1,128)} %bitcast.15), calls=%async_computation.9 | async-start | bytes 589824 | tf_op jit(solution)/shard_map/all_to_all | solution.py:57
  378.2 10.1 %all-to-all-done.8 = f32[64,1,1152]{2,1,0:T(1,128)S(1)} async-done(((f32[64,1,1152]{2,1,0:T(1,128)}), f32[64,1,1152]{2,1,0:T(1,128)S(1)}, u32[]{:S(2)}, u32[]{:S(2)}) %all-to-all-start.8) | async-done | bytes 294944 | tf_op jit(solution)/shard_map/all_to_all | solution.py:57
  389.7 5.7 %all-to-all-start.6 = ((bf16[16,48,1024]{2,1,0:T(8,128)(2,1)}), bf16[16,48,1024]{2,1,0:T(8,128)(2,1)S(1)}, u32[]{:S(2)}, u32[]{:S(2)}) async-start(bf16[16,48,1024]{2,1,0:T(8,128)(2,1)} %broadcast_in_dim.62), calls=%async_computation.7 | async-start | bytes 3145728 | tf_op jit(solution)/shard_map/all_to_all | solution.py:33
  395.6 35.4 %all-to-all-done.6 = bf16[16,48,1024]{2,1,0:T(8,128)(2,1)S(1)} async-done(((bf16[16,48,1024]{2,1,0:T(8,128)(2,1)}), bf16[16,48,1024]{2,1,0:T(8,128)(2,1)S(1)}, u32[]{:S(2)}, u32[]{:S(2)}) %all-to-all-start.6) | async-done | bytes 1572896 | tf_op jit(solution)/shard_map/all_to_all | solution.py:33
  431.8 7.0 %all-to-all-start.9 = ((f32[64,1,1152]{2,1,0:T(1,128)}), f32[64,1,1152]{2,1,0:T(1,128)S(1)}, u32[]{:S(2)}, u32[]{:S(2)}) async-start(f32[64,1,1152]{2,1,0:T(1,128)} %broadcast_in_dim.64), calls=%async_computation.10 | async-start | bytes 589824 | tf_op jit(solution)/shard_map/all_to_all | solution.py:33
  440.6 8.8 %all-to-all-done.9 = f32[64,1,1152]{2,1,0:T(1,128)S(1)} async-done(((f32[64,1,1152]{2,1,0:T(1,128)}), f32[64,1,1152]{2,1,0:T(1,128)S(1)}, u32[]{:S(2)}, u32[]{:S(2)}) %all-to-all-start.9) | async-done | bytes 294944 | tf_op jit(solution)/shard_map/all_to_all | solution.py:33
  451.3 3.8 all-to-all-start.7
  465.5 20.7 %all-to-all-done.7 = bf16[4,320,1024]{2,1,0:T(8,128)(2,1)S(1)} async-done(((bf16[4,320,1024]{2,1,0:T(8,128)(2,1)}), bf16[4,320,1024]{2,1,0:T(8,128)(2,1)S(1)}, u32[]{:S(2)}, u32[]{:S(2)}) %all-to-all-start.7) | async-done | bytes 2621472 | tf_op jit(solution)/shard_map/all_to_all | solution.py:33
  (126 shorter events, 42.9 us)
Async XLA Ops:
  7.2 12.9 %copy-start.15 = (s32[1,16,16]{2,1,0:T(8,128)S(1)}, s32[1,16,16]{2,1,0:T(8,128)}, u32[]{:S(2)}) copy-start(s32[1,16,16]{2,1,0:T(8,128)} %param.19) | copy-start | bytes 3076
  7.2 12.9 %copy-start.16 = (s32[1,16,16]{2,1,0:T(8,128)S(1)}, s32[1,16,16]{2,1,0:T(8,128)}, u32[]{:S(2)}) copy-start(s32[1,16,16]{2,1,0:T(8,128)} %param.20) | copy-start | bytes 3076
  11.5 45.0 %all-to-all-start = ((bf16[16,48,1024]{2,1,0:T(8,128)(2,1)}), bf16[16,48,1024]{2,1,0:T(8,128)(2,1)S(1)}, u32[]{:S(2)}, u32[]{:S(2)}) async-start(bf16[16,48,1024]{2,1,0:T(8,128)(2,1)} %bitcast.59), calls=%async_computation | async-start | bytes 3145728 | tf_op jit(solution)/shard_map/all_to_all | solution.py:18
  21.4 311.3 %copy-start.17 = (s32[96]{0:T(128)}, s32[96]{0:T(128)S(1)}, u32[]{:S(2)}) copy-start(s32[96]{0:T(128)S(1)} %get-tuple-element.41) | copy-start | bytes 1156
  21.4 311.3 %copy-start.18 = (pred[96]{0:T(512)(128)(4,1)}, pred[96]{0:T(512)(128)(4,1)S(1)}, u32[]{:S(2)}) copy-start(pred[96]{0:T(512)(128)(4,1)S(1)} %get-tuple-element.39) | copy-start | bytes 292
  57.8 13.1 %all-to-all-start.1 = ((bf16[16,6,1024]{2,1,0:T(8,128)(2,1)}), bf16[16,6,1024]{2,1,0:T(8,128)(2,1)S(1)}, u32[]{:S(2)}, u32[]{:S(2)}) async-start(bf16[16,6,1024]{2,1,0:T(8,128)(2,1)} %reshape.199), calls=%async_computation.1 | async-start | bytes 524288 | tf_op jit(solution)/shard_map/all_to_all | solution.py:144
  74.8 12.6 %copy-start.8 = (bf16[2048,64]{0,1:T(8,128)(2,1)S(1)}, bf16[2048,64]{0,1:T(8,128)(2,1)}, u32[]{:S(2)}) copy-start(bf16[2048,64]{0,1:T(8,128)(2,1)} %param.17) | copy-start | bytes 786436
  74.8 12.9 %copy-start.6 = (bf16[2048,128]{1,0:T(8,128)(2,1)S(1)}, bf16[2048,128]{1,0:T(8,128)(2,1)}, u32[]{:S(2)}) copy-start(bf16[2048,128]{1,0:T(8,128)(2,1)} %param.16) | copy-start | bytes 1572868
  74.8 225.1 %all-to-all-start.2 = ((bf16[8,256,1024]{1,2,0:T(8,128)(2,1)}), bf16[8,256,1024]{1,2,0:T(8,128)(2,1)}, u32[]{:S(2)}, u32[]{:S(2)}) async-start(bf16[8,256,1024]{1,2,0:T(8,128)(2,1)} %stack.6), calls=%async_computation.2 | async-start | bytes 8388608 | tf_op jit(solution)/shard_map/all_to_all | solution.py:153
  87.3 60.5 %all-gather.2.cloned.1.call-start = ((), (), s32[]{:S(2)}) async-start(), calls=%async_computation.11 | async-start | bytes 5242880 | tf_op jit(solution)/shard_map/all_gather | solution.py:28
  88.9 265.0 %reduce-scatter.2.cloned.1.call-start = ((), (), s32[]{:S(2)}) async-start(), calls=%async_computation.12 | async-start | bytes 1769472 | tf_op jit(solution)/shard_map/reduce_scatter | solution.py:200
  151.6 151.7 %copy-start.12 = (f32[8192]{0:T(1024)S(1)}, f32[8192]{0:T(1024)}, u32[]{:S(2)}) copy-start(f32[8192]{0:T(1024)} %param.15) | copy-start | bytes 98308
  307.7 24.2 %copy-start.4 = (f32[256,64]{0,1:T(8,128)}, f32[256,64]{0,1:T(8,128)S(1)}, u32[]{:S(2)}) copy-start(f32[256,64]{0,1:T(8,128)S(1)} %fusion.70) | copy-start | bytes 196612
  327.1 24.7 %all-to-all-start.4 = ((bf16[8,256,64]{1,2,0:T(8,128)(2,1)}), bf16[8,256,64]{1,2,0:T(8,128)(2,1)S(1)}, u32[]{:S(2)}, u32[]{:S(2)}) async-start(bf16[8,256,64]{1,2,0:T(8,128)(2,1)} %broadcast_in_dim.61), calls=%async_computation.5 | async-start | bytes 524288 | tf_op jit(solution)/shard_map/all_to_all | solution.py:33
  331.1 22.8 %slice-start = ((bf16[8192,192]{1,0:T(8,128)(2,1)}), bf16[8192,64]{1,0:T(8,128)(2,1)S(1)}, s32[]{:S(2)}) async-start(bf16[8192,192]{1,0:T(8,128)(2,1)} %all-gather.2.cloned.1.call-done), calls=%async_computation.13 | async-start | bytes 4194304 | tf_op jit(solution)/shard_map/split | solution.py:28
  353.9 23.8 %copy-start.20 = (s32[16]{0:T(128)S(1)}, s32[16]{0:T(128)}, u32[]{:S(2)}) copy-start(s32[16]{0:T(128)} %copy-done.19) | copy-start | bytes 196
  353.9 23.9 %copy-start.14 = (s32[16]{0:T(128)S(1)}, s32[16]{0:T(128)}, u32[]{:S(2)}) copy-start(s32[16]{0:T(128)} %copy-done.13) | copy-start | bytes 196
  356.2 12.5 %all-to-all-start.5 = ((bf16[16,6,1024]{2,1,0:T(8,128)(2,1)}), bf16[16,6,1024]{2,1,0:T(8,128)(2,1)S(1)}, u32[]{:S(2)}, u32[]{:S(2)}) async-start(bf16[16,6,1024]{2,1,0:T(8,128)(2,1)} %reshape.200), calls=%async_computation.6 | async-start | bytes 524288 | tf_op jit(solution)/shard_map/all_to_all | solution.py:216
  368.7 19.6 %all-to-all-start.8 = ((f32[64,1,1152]{2,1,0:T(1,128)}), f32[64,1,1152]{2,1,0:T(1,128)S(1)}, u32[]{:S(2)}, u32[]{:S(2)}) async-start(f32[64,1,1152]{2,1,0:T(1,128)} %bitcast.15), calls=%async_computation.9 | async-start | bytes 589824 | tf_op jit(solution)/shard_map/all_to_all | solution.py:57
  389.7 41.2 %all-to-all-start.6 = ((bf16[16,48,1024]{2,1,0:T(8,128)(2,1)}), bf16[16,48,1024]{2,1,0:T(8,128)(2,1)S(1)}, u32[]{:S(2)}, u32[]{:S(2)}) async-start(bf16[16,48,1024]{2,1,0:T(8,128)(2,1)} %broadcast_in_dim.62), calls=%async_computation.7 | async-start | bytes 3145728 | tf_op jit(solution)/shard_map/all_to_all | solution.py:33
  431.8 17.6 %all-to-all-start.9 = ((f32[64,1,1152]{2,1,0:T(1,128)}), f32[64,1,1152]{2,1,0:T(1,128)S(1)}, u32[]{:S(2)}, u32[]{:S(2)}) async-start(f32[64,1,1152]{2,1,0:T(1,128)} %broadcast_in_dim.64), calls=%async_computation.10 | async-start | bytes 589824 | tf_op jit(solution)/shard_map/all_to_all | solution.py:33
  451.3 3.8 copy-start.5
  451.3 3.8 copy-start.9
  451.3 35.0 %all-to-all-start.7 = ((bf16[4,320,1024]{2,1,0:T(8,128)(2,1)}), bf16[4,320,1024]{2,1,0:T(8,128)(2,1)S(1)}, u32[]{:S(2)}, u32[]{:S(2)}) async-start(bf16[4,320,1024]{2,1,0:T(8,128)(2,1)} %broadcast_in_dim.63), calls=%async_computation.8 | async-start | bytes 5242880 | tf_op jit(solution)/shard_map/all_to_all | solution.py:33
  (11 other events, 16.8 us)
Sparse Core Ops, SparseCore 0:
  90.8 56.9 all-gather.1
  151.7 125.5 reduce-scatter.1
